TPU v7x, 32 devices: a whole 2x2x4 slice. The times are simulated.
32 devices in a mesh: group: 2 (over x), tm: 16 (over z, y, core).
Axes of the slice: x: 2, y: 2, z: 4, core: 2. Of those that a mesh axis runs over, the one named last changes fastest.
Arguments:
- patches: bfloat16 [32, 1024, 128], P(('group', 'tm')), parts along dimension 0, may hold values from -6 to 6
- classes: int32 [32], P(('group', 'tm')), parts along dimension 0, may hold values from 0 to 15
- dilations: int32 [4], replicated, may hold values from 1 to 4, as said below
- enc_weight: bfloat16 [128, 256], replicated, may hold values from -0.5 to 0.5
- cond_table: bfloat16 [16, 256], replicated, may hold values from -3 to 3
- temp_weight: bfloat16 [4, 512, 256], replicated, may hold values from -0.25 to 0.25
- dec_weight: bfloat16 [256, 128], replicated, may hold values from -0.375 to 0.375
- cotangent: bfloat16 [32, 1024, 128], P(('group', 'tm')), parts along dimension 0, may hold values from -0.125 to 0.125
Outputs:
- decoded: bfloat16 [32, 1024, 128], P(('group', 'tm')), parts along dimension 0
- grad_encoder: float32 [256, 256], P(('group', 'tm')), parts along dimension 0
- grad_temporal: float32 [8, 512, 256], P('group', 'tm'), parts along dimension 0
- grad_decoder: float32 [512, 128], P(('group', 'tm')), parts along dimension 0
There are 2 independent parts, one for each index of `group`. A program takes and returns all parts, laid end to end along the dimension named above; an argument that names none is the same for every part. Nothing has to cross between parts.
Inputs may be any that keep to these rules, and one draw needn't show every extreme that they name: `dilations`: every layer's dilation lies in 1 to 4, and some layer's is exactly 4.
All inputs are finite; a program needn't handle non-finite values.
Results may differ from a plain program's by a relative error of at most 0.009.
Values may be sent and summed in bfloat16 or wider, within the bound.
A program may use at most 64 MiB of HBM per device.

v0:
```python
import jax
import jax.numpy as jnp
from jax import lax
from jax.sharding import PartitionSpec as P


def shift_late(values, spacing, margin):
    filler = jnp.zeros((margin,) + values.shape[1:], values.dtype)
    padded = jnp.concatenate([filler, values], axis=0)
    return lax.dynamic_slice_in_dim(padded, margin - spacing, values.shape[0], 0)


def shift_early(values, spacing, margin):
    filler = jnp.zeros((margin,) + values.shape[1:], values.dtype)
    padded = jnp.concatenate([values, filler], axis=0)
    return lax.dynamic_slice_in_dim(padded, spacing, values.shape[0], 0)


def encode_rows(patch_rows, frame_kinds, enc_weight, cond_table):
    kinds = cond_table.shape[0]
    onehot = (frame_kinds[:, None] == jnp.arange(kinds, dtype=jnp.int32)[None, :]).astype(
        jnp.bfloat16
    )
    embedded = jnp.dot(onehot, cond_table, preferred_element_type=jnp.float32)
    start = jnp.einsum("tpc,cd->tpd", patch_rows, enc_weight, preferred_element_type=jnp.float32)
    return (start + embedded[:, None, :]).astype(jnp.bfloat16)


def shards(patches, classes, dilations, enc_weight, cond_table, temp_weight, dec_weight, cotangent):
    layers = temp_weight.shape[0]
    width = temp_weight.shape[2]
    start = encode_rows(patches, classes, enc_weight, cond_table)
    latent = lax.all_to_all(start, "tm", split_axis=1, concat_axis=0, tiled=True)
    margin = latent.shape[0] // 4
    saved = []
    for layer in range(layers):
        joined = jnp.concatenate([latent, shift_late(latent, dilations[layer], margin)], axis=-1)
        pre_act = jnp.einsum(
            "tpk,kd->tpd", joined, temp_weight[layer], preferred_element_type=jnp.float32
        )
        saved.append((joined, pre_act))
        latent = (latent.astype(jnp.float32) + jax.nn.silu(pre_act)).astype(jnp.bfloat16)
    final = lax.all_to_all(latent, "tm", split_axis=0, concat_axis=1, tiled=True)
    decoded = jnp.einsum(
        "fpd,dc->fpc", final, dec_weight, preferred_element_type=jnp.float32
    ).astype(jnp.bfloat16)
    dec_term = jnp.einsum("fpd,fpc->dc", final, cotangent, preferred_element_type=jnp.float32)
    upstream = jnp.einsum(
        "fpc,dc->fpd", cotangent, dec_weight, preferred_element_type=jnp.float32
    ).astype(jnp.bfloat16)
    carried = lax.all_to_all(upstream, "tm", split_axis=1, concat_axis=0, tiled=True)
    layer_terms = [None] * layers
    for layer in reversed(range(layers)):
        joined, pre_act = saved[layer]
        gate_value = jax.nn.sigmoid(pre_act)
        dpre = (
            carried.astype(jnp.float32) * gate_value * (1.0 + pre_act * (1.0 - gate_value))
        ).astype(jnp.bfloat16)
        layer_term = jnp.einsum("tpk,tpd->kd", joined, dpre, preferred_element_type=jnp.float32)
        layer_terms[layer] = layer_term
        returned = jnp.einsum(
            "tpd,kd->tpk", dpre, temp_weight[layer], preferred_element_type=jnp.float32
        )
        carried = (
            carried.astype(jnp.float32)
            + returned[..., :width]
            + shift_early(returned[..., width:], dilations[layer], margin)
        ).astype(jnp.bfloat16)
    stacked = jnp.stack(layer_terms)
    grad_temporal = lax.psum_scatter(stacked, "tm", scatter_dimension=1, tiled=True)
    carried_frames = lax.all_to_all(carried, "tm", split_axis=0, concat_axis=1, tiled=True)
    enc_term = jnp.einsum(
        "fpc,fpd->cd", patches, carried_frames, preferred_element_type=jnp.float32
    )
    grad_encoder, grad_decoder = (
        lax.psum_scatter(enc_term, "tm", scatter_dimension=0, tiled=True),
        lax.psum_scatter(dec_term, "tm", scatter_dimension=0, tiled=True),
    )
    return (decoded, grad_encoder, grad_temporal, grad_decoder)


def solution(mesh):
    in_specs = (
        P(("group", "tm"), None, None),
        P(("group", "tm")),
        P(),
        P(),
        P(),
        P(),
        P(),
        P(("group", "tm"), None, None),
    )
    out_specs = (
        P(("group", "tm"), None, None),
        P(("group", "tm"), None),
        P("group", "tm", None),
        P(("group", "tm"), None),
    )
    return jax.shard_map(shards, mesh=mesh, in_specs=in_specs, out_specs=out_specs, check_vma=False)
```

profile of v0, /device:TPU:0, one launch (start us, length us, event | category | flops | bytes accessed | tf_op | source)
XLA Modules:
  0.0 280.7 jit_solution(17788033939454266709)
XLA Ops:
  7.9 0.8 fusion.47
  8.7 1.2 fusion.2
  9.9 0.8 copy.26
  10.7 0.5 broadcast.31
  11.3 3.8 %reduce.1 = bf16[1024,256]{1,0:T(8,128)(2,1)S(1)} reduce(bf16[1024,1,256]{2,1,0:T(2,128)(2,1)S(1)} %bitcast.97, bf16[]{:T(256)} %broadcast.31), dimensions={1}, to_apply=%bitcast.92.reduce_sub_computation | reduce | bytes 1048578
  15.1 0.9 reshape.78
  16.0 7.4 %all-to-all-start = ((bf16[16,2,8192]{2,1,0:T(2,128)(2,1)}), bf16[16,2,8192]{2,1,0:T(2,128)(2,1)S(1)}, u32[]{:S(2)}, u32[]{:S(2)}) async-start(bf16[16,2,8192]{2,1,0:T(2,128)(2,1)} %reshape.78), calls=%async_computation | async-start | bytes 1048576 | tf_op jit(solution)/shard_map/all_to_all | solution.py:33
  23.5 0.3 fusion.1
  23.8 0.8 copy.25
  24.6 3.8 %reduce = bf16[1024,256]{1,0:T(8,128)(2,1)S(1)} reduce(bf16[1024,1,256]{2,1,0:T(2,128)(2,1)S(1)} %bitcast.98, bf16[]{:T(256)} %broadcast.31), dimensions={1}, to_apply=%bitcast.91.reduce_sub_computation | reduce | bytes 1048578
  28.4 0.9 reshape.76
  29.4 8.5 %all-to-all-done = bf16[16,2,8192]{2,1,0:T(2,128)(2,1)S(1)} async-done(((bf16[16,2,8192]{2,1,0:T(2,128)(2,1)}), bf16[16,2,8192]{2,1,0:T(2,128)(2,1)S(1)}, u32[]{:S(2)}, u32[]{:S(2)}) %all-to-all-start) | async-done | bytes 524320 | tf_op jit(solution)/shard_map/all_to_all | solution.py:33
  37.9 4.1 %all-to-all-start.2 = ((bf16[16,2,8192]{2,1,0:T(2,128)(2,1)}), bf16[16,2,8192]{2,1,0:T(2,128)(2,1)S(1)}, u32[]{:S(2)}, u32[]{:S(2)}) async-start(bf16[16,2,8192]{2,1,0:T(2,128)(2,1)} %reshape.76), calls=%async_computation.2 | async-start | bytes 1048576 | tf_op jit(solution)/shard_map/all_to_all | solution.py:51
  42.0 0.6 fusion.66
  55.6 0.5 reshape.79
  56.5 0.5 reshape.77
  57.2 2.6 add_convert_fusion.3
  59.9 1.4 add_convert_fusion.2
  61.4 1.4 add_convert_fusion.1
  62.9 1.5 multiply_convert_fusion
  64.4 5.7 %all-to-all-start.1 = ((bf16[16,64,256]{2,1,0:T(8,128)(2,1)}), bf16[16,64,256]{2,1,0:T(8,128)(2,1)S(1)}, u32[]{:S(2)}, u32[]{:S(2)}) async-start(bf16[16,64,256]{2,1,0:T(8,128)(2,1)} %get-tuple-element.17), calls=%async_computation.1 | async-start | bytes 1048576 | tf_op jit(solution)/shard_map/all_to_all | solution.py:43
  70.1 1.4 fusion.25
  71.7 0.3 fusion.5
  72.0 0.9 copy-done.19
  72.9 0.3 copy-done.24
  73.2 0.6 fusion.28
  74.2 0.9 copy-done.23
  75.2 0.6 fusion.31
  75.9 0.3 fusion.9
  76.2 0.9 copy-done.21
  77.2 0.6 fusion.34
  77.9 1.1 fusion.11
  79.1 1.5 convolution_bitcast_fusion.1
  80.6 4.0 %all-to-all-done.1 = bf16[16,64,256]{2,1,0:T(8,128)(2,1)S(1)} async-done(((bf16[16,64,256]{2,1,0:T(8,128)(2,1)}), bf16[16,64,256]{2,1,0:T(8,128)(2,1)S(1)}, u32[]{:S(2)}, u32[]{:S(2)}) %all-to-all-start.1) | async-done | bytes 524320 | tf_op jit(solution)/shard_map/all_to_all | solution.py:43
  84.6 4.1 %all-to-all-start.3 = ((bf16[16,64,256]{2,1,0:T(8,128)(2,1)}), bf16[16,64,256]{2,1,0:T(8,128)(2,1)S(1)}, u32[]{:S(2)}, u32[]{:S(2)}) async-start(bf16[16,64,256]{2,1,0:T(8,128)(2,1)} %fusion.11), calls=%async_computation.3 | async-start | bytes 1048576 | tf_op jit(solution)/shard_map/all_to_all | solution.py:71
  88.8 3.1 %convolution_bitcast_fusion.2 = f32[1,512,256]{2,1,0:T(8,128)} fusion(bf16[16,64,256]{2,1,0:T(8,128)(2,1)} %copy-done.7, bf16[16,64,256]{2,1,0:T(8,128)(2,1)} %copy-done.6, bf16[16,64,256]{2,1,0:T(8,128)(2,1)S(1)} %fusion.7, f32[16,64,256]{2,1,0:T(8,128)} %get-tuple-element.25), kind=kOutput, calls=%fused_computation.18 | convolution fusion | flops 273154048 | bytes 3145728 | tf_op jit(solution)/shard_map/tpk,tpd->kd/dot_general | solution.py:59
  91.9 1.5 convolution_bitcast_fusion.3
  93.4 1.0 fusion.22
  94.5 8.7 %all-to-all-done.3 = bf16[16,64,256]{2,1,0:T(8,128)(2,1)S(1)} async-done(((bf16[16,64,256]{2,1,0:T(8,128)(2,1)}), bf16[16,64,256]{2,1,0:T(8,128)(2,1)S(1)}, u32[]{:S(2)}, u32[]{:S(2)}) %all-to-all-start.3) | async-done | bytes 524320 | tf_op jit(solution)/shard_map/all_to_all | solution.py:71
  103.2 0.3 convolution_bitcast_fusion.4
  103.5 0.8 copy.19
  104.4 0.5 convolution_bitcast_fusion
  104.9 0.5 copy-done.14
  105.7 1.5 pad_maximum_fusion
  107.2 1.0 fusion.3
  108.2 42.8 %reduce-scatter.8.cloned.1.call-done = f32[16,128]{1,0:T(8,128)} async-done(((f32[256,128]{1,0:T(8,128)}), f32[16,128]{1,0:T(8,128)}) %reduce-scatter.8.cloned.1.call-update) | async-done | bytes 8208 | tf_op jit(solution)/shard_map/reduce_scatter | solution.py:77
  151.0 58.2 %reduce-scatter.10.cloned.1.call-done = f32[8,256]{1,0:T(8,128)} async-done(((f32[128,256]{1,0:T(8,128)}), f32[8,256]{1,0:T(8,128)}) %reduce-scatter.10.cloned.1.call-update) | async-done | bytes 8208
  209.2 65.0 %reduce-scatter.6.cloned.1.call-done = f32[4,32,256]{2,1,0:T(8,128)} async-done(((f32[4,512,256]{2,1,0:T(8,128)}), f32[4,32,256]{2,1,0:T(8,128)}) %reduce-scatter.6.cloned.1.call-update) | async-done | bytes 131088 | tf_op jit(solution)/shard_map/reduce_scatter | solution.py:70
  (63 shorter events, 2.1 us)
Async XLA Ops:
  7.2 16.3 %copy-start = (bf16[1,1024,128]{2,1,0:T(8,128)(2,1)S(1)}, bf16[1,1024,128]{2,1,0:T(8,128)(2,1)}, u32[]{:S(2)}) copy-start(bf16[1,1024,128]{2,1,0:T(8,128)(2,1)} %param.15) | copy-start | bytes 786436
  10.7 12.7 %copy-start.17 = (bf16[256,128]{1,0:T(8,128)(2,1)S(1)}, bf16[256,128]{1,0:T(8,128)(2,1)}, u32[]{:S(2)}) copy-start(bf16[256,128]{1,0:T(8,128)(2,1)} %param.14) | copy-start | bytes 196612
  16.0 21.9 %all-to-all-start = ((bf16[16,2,8192]{2,1,0:T(2,128)(2,1)}), bf16[16,2,8192]{2,1,0:T(2,128)(2,1)S(1)}, u32[]{:S(2)}, u32[]{:S(2)}) async-start(bf16[16,2,8192]{2,1,0:T(2,128)(2,1)} %reshape.78), calls=%async_computation | async-start | bytes 1048576 | tf_op jit(solution)/shard_map/all_to_all | solution.py:33
  24.6 17.4 %copy-start.20 = (s32[4]{0:T(128)S(1)}, s32[4]{0:T(128)}, u32[]{:S(2)}) copy-start(s32[4]{0:T(128)} %param.10) | copy-start | bytes 52
  37.9 18.6 %all-to-all-start.2 = ((bf16[16,2,8192]{2,1,0:T(2,128)(2,1)}), bf16[16,2,8192]{2,1,0:T(2,128)(2,1)S(1)}, u32[]{:S(2)}, u32[]{:S(2)}) async-start(bf16[16,2,8192]{2,1,0:T(2,128)(2,1)} %reshape.76), calls=%async_computation.2 | async-start | bytes 1048576 | tf_op jit(solution)/shard_map/all_to_all | solution.py:51
  57.2 2.6 copy-start.4
  57.2 2.7 copy-start.18
  59.8 3.0 %copy-start.6 = (bf16[16,64,256]{2,1,0:T(8,128)(2,1)}, bf16[16,64,256]{2,1,0:T(8,128)(2,1)S(1)}, u32[]{:S(2)}) copy-start(bf16[16,64,256]{2,1,0:T(8,128)(2,1)S(1)} %get-tuple-element.22) | copy-start | bytes 1572868
  59.9 3.0 %copy-start.7 = (bf16[16,64,256]{2,1,0:T(8,128)(2,1)}, bf16[16,64,256]{2,1,0:T(8,128)(2,1)S(1)}, u32[]{:S(2)}) copy-start(bf16[16,64,256]{2,1,0:T(8,128)(2,1)S(1)} %pad_dynamic-slice_fusion.6) | copy-start | bytes 1572868
  61.3 1.5 copy-start.8
  61.4 1.5 copy-start.10
  62.9 1.5 copy-start.2
  64.4 7.2 %copy-start.12 = (bf16[16,64,256]{2,1,0:T(8,128)(2,1)}, bf16[16,64,256]{2,1,0:T(8,128)(2,1)S(1)}, u32[]{:S(2)}) copy-start(bf16[16,64,256]{2,1,0:T(8,128)(2,1)S(1)} %get-tuple-element.16) | copy-start | bytes 1572868
  64.4 20.2 %all-to-all-start.1 = ((bf16[16,64,256]{2,1,0:T(8,128)(2,1)}), bf16[16,64,256]{2,1,0:T(8,128)(2,1)S(1)}, u32[]{:S(2)}, u32[]{:S(2)}) async-start(bf16[16,64,256]{2,1,0:T(8,128)(2,1)} %get-tuple-element.17), calls=%async_computation.1 | async-start | bytes 1048576 | tf_op jit(solution)/shard_map/all_to_all | solution.py:43
  71.7 1.2 copy-start.19
  71.7 1.5 copy-start.24
  74.0 1.2 copy-start.23
  75.9 1.2 copy-start.21
  77.9 1.1 copy-start.9
  77.9 1.2 copy-start.11
  84.6 18.6 %all-to-all-start.3 = ((bf16[16,64,256]{2,1,0:T(8,128)(2,1)}), bf16[16,64,256]{2,1,0:T(8,128)(2,1)S(1)}, u32[]{:S(2)}, u32[]{:S(2)}) async-start(bf16[16,64,256]{2,1,0:T(8,128)(2,1)} %fusion.11), calls=%async_computation.3 | async-start | bytes 1048576 | tf_op jit(solution)/shard_map/all_to_all | solution.py:71
  88.7 62.3 %reduce-scatter.8.cloned.1.call-start = ((), (), s32[]{:S(2)}) async-start(), calls=%async_computation.8 | async-start | bytes 139264 | tf_op jit(solution)/shard_map/reduce_scatter | solution.py:77
  88.8 3.2 %copy-start.5 = (bf16[16,64,256]{2,1,0:T(8,128)(2,1)S(1)}, bf16[16,64,256]{2,1,0:T(8,128)(2,1)}, u32[]{:S(2)}) copy-start(bf16[16,64,256]{2,1,0:T(8,128)(2,1)} %copy-done.4) | copy-start | bytes 1572868
  88.8 3.2 %copy-start.22 = (f32[16,64,256]{2,1,0:T(8,128)S(1)}, f32[16,64,256]{2,1,0:T(8,128)}, u32[]{:S(2)}) copy-start(f32[16,64,256]{2,1,0:T(8,128)} %get-tuple-element.23) | copy-start | bytes 3145732
  91.9 11.2 %copy-start.1 = (bf16[1,1024,128]{2,1,0:T(8,128)(2,1)S(1)}, bf16[1,1024,128]{2,1,0:T(8,128)(2,1)}, u32[]{:S(2)}) copy-start(bf16[1,1024,128]{2,1,0:T(8,128)(2,1)} %param.8) | copy-start | bytes 786436
  93.4 10.9 %copy-start.3 = (bf16[16,64,256]{2,1,0:T(8,128)(2,1)S(1)}, bf16[16,64,256]{2,1,0:T(8,128)(2,1)}, u32[]{:S(2)}) copy-start(bf16[16,64,256]{2,1,0:T(8,128)(2,1)} %copy-done.2) | copy-start | bytes 1572868
  93.4 10.9 %copy-start.13 = (bf16[16,64,256]{2,1,0:T(8,128)(2,1)S(1)}, bf16[16,64,256]{2,1,0:T(8,128)(2,1)}, u32[]{:S(2)}) copy-start(bf16[16,64,256]{2,1,0:T(8,128)(2,1)} %copy-done.12) | copy-start | bytes 1572868
  94.5 114.7 %reduce-scatter.10.cloned.1.call-start = ((), (), s32[]{:S(2)}) async-start(), calls=%async_computation.9 | async-start | bytes 139264
  104.3 1.0 copy-start.14
  104.3 169.9 %reduce-scatter.6.cloned.1.call-start = ((), (), s32[]{:S(2)}) async-start(), calls=%async_computation.7 | async-start | bytes 2228224 | tf_op jit(solution)/shard_map/reduce_scatter | solution.py:70
  104.4 1.1 copy-start.15
  104.4 1.3 copy-start.16
Sparse Core Ops, SparseCore 0:
  94.6 56.3 reduce-scatter.7
  155.0 54.0 reduce-scatter.9
  213.5 60.6 reduce-scatter.5
where the time goes:
time: 282 us; the launch traced here: 281 us
  waiting for transfers between devices  187 us (66%)
  between operations  27.8 us (10%)
  matrix products  21.5 us (8%)
  starting transfers between devices  21.5 us (8%)
  local copies, waits for them, and re-layouts  11.4 us (4%)
  other arithmetic  11.1 us (4%)
    reduce_scatter x1, waiting for transfers between devices, shards(): lax.psum_scatter(stacked, 'tm', scatter_dimension=1, tiled=True)  65 us
    unnamed x4, waiting for transfers between devices  58.2 us
    reduce_scatter x1, waiting for transfers between devices, shards(): lax.psum_scatter(dec_term, 'tm', scatter_dimension=0, tiled=True)  42.8 us
    all_to_all x1, waiting for transfers between devices, shards(): lax.all_to_all(carried, 'tm', split_axis=0, concat_axis=1, tiled=True)  8.67 us
    all_to_all x1, waiting for transfers between devices, shards(): lax.all_to_all(start, 'tm', split_axis=1, concat_axis=0, tiled=True)  8.54 us
    unnamed x58, local copies, waits for them, and re-layouts  8.44 us
    unnamed x2, other arithmetic  7.66 us
    all_to_all x1, starting transfers between devices, shards(): lax.all_to_all(start, 'tm', split_axis=1, concat_axis=0, tiled=True)  7.4 us
  transfers between devices with their start and end apart: 7, of which 7 were waited for; matrix products, arithmetic and copies ran while one was open for 9% of the time, Pallas kernels for 0%

commit v1 on v0

--- a/solution.py
+++ b/solution.py
@@ -40,7 +40,10 @@
         )
         saved.append((joined, pre_act))
         latent = (latent.astype(jnp.float32) + jax.nn.silu(pre_act)).astype(jnp.bfloat16)
-    final = lax.all_to_all(latent, "tm", split_axis=0, concat_axis=1, tiled=True)
+    final = jnp.concatenate(
+        lax.all_to_all(jnp.stack(jnp.split(latent, lax.axis_size("tm"), axis=0)), "tm", 0, 0),
+        axis=1,
+    )
     decoded = jnp.einsum(
         "fpd,dc->fpc", final, dec_weight, preferred_element_type=jnp.float32
     ).astype(jnp.bfloat16)

time: 282 us -> 292 us (1.035)
  local copies, waits for them, and re-layouts: 11.4 us -> 21.2 us
    unnamed x58 -> x73, local copies, waits for them, and re-layouts: 8.44 us -> 17.6 us
  transfers between devices with their start and end apart: 7 -> 7, of which waited for: 7 -> 7; matrix products, arithmetic and copies ran while one was open for 9% -> 8% of each run, Pallas kernels for 0% -> 0%
where the time goes in v1:
time: 292 us; the launch traced here: 291 us
  waiting for transfers between devices  187 us (64%)
  between operations  27.8 us (10%)
  matrix products  21.6 us (7%)
  starting transfers between devices  21.5 us (7%)
  local copies, waits for them, and re-layouts  21.2 us (7%)
  other arithmetic  11.1 us (4%)
    reduce_scatter x1, waiting for transfers between devices, shards(): lax.psum_scatter(stacked, 'tm', scatter_dimension=1, tiled=True)  64.9 us
    unnamed x4, waiting for transfers between devices  58.3 us
    reduce_scatter x1, waiting for transfers between devices, shards(): lax.psum_scatter(dec_term, 'tm', scatter_dimension=0, tiled=True)  42.8 us
    unnamed x73, local copies, waits for them, and re-layouts  17.6 us
    all_to_all x1, waiting for transfers between devices, shards(): lax.all_to_all(carried, 'tm', split_axis=0, concat_axis=1, tiled=True)  8.67 us
    all_to_all x1, waiting for transfers between devices, shards(): lax.all_to_all(start, 'tm', split_axis=1, concat_axis=0, tiled=True)  8.54 us
    unnamed x2, other arithmetic  7.66 us
    all_to_all x1, starting transfers between devices, shards(): lax.all_to_all(start, 'tm', split_axis=1, concat_axis=0, tiled=True)  7.4 us
  transfers between devices with their start and end apart: 7, of which 7 were waited for; matrix products, arithmetic and copies ran while one was open for 8% of the time, Pallas kernels for 0%

profile of v1, /device:TPU:0, one launch (start us, length us, event | category | flops | bytes accessed | tf_op | source)
XLA Modules:
  0.0 290.5 jit_solution(13496469032162262667)
XLA Ops:
  7.9 0.8 fusion.47
  8.7 1.2 fusion.2
  9.9 0.8 copy.26
  11.3 3.8 %reduce.1 = bf16[1024,256]{1,0:T(8,128)(2,1)S(1)} reduce(bf16[1024,1,256]{2,1,0:T(2,128)(2,1)S(1)} %bitcast.161, bf16[]{:T(256)} %broadcast.31), dimensions={1}, to_apply=%bitcast.156.reduce_sub_computation | reduce | bytes 1048578
  15.1 0.9 reshape.76
  16.0 7.4 %all-to-all-start = ((bf16[16,2,8192]{2,1,0:T(2,128)(2,1)}), bf16[16,2,8192]{2,1,0:T(2,128)(2,1)S(1)}, u32[]{:S(2)}, u32[]{:S(2)}) async-start(bf16[16,2,8192]{2,1,0:T(2,128)(2,1)} %reshape.76), calls=%async_computation | async-start | bytes 1048576 | tf_op jit(solution)/shard_map/all_to_all | solution.py:33
  23.8 0.8 copy.25
  24.6 3.8 %reduce = bf16[1024,256]{1,0:T(8,128)(2,1)S(1)} reduce(bf16[1024,1,256]{2,1,0:T(2,128)(2,1)S(1)} %bitcast.162, bf16[]{:T(256)} %broadcast.31), dimensions={1}, to_apply=%bitcast.155.reduce_sub_computation | reduce | bytes 1048578
  28.4 0.9 reshape.74
  29.4 8.5 %all-to-all-done = bf16[16,2,8192]{2,1,0:T(2,128)(2,1)S(1)} async-done(((bf16[16,2,8192]{2,1,0:T(2,128)(2,1)}), bf16[16,2,8192]{2,1,0:T(2,128)(2,1)S(1)}, u32[]{:S(2)}, u32[]{:S(2)}) %all-to-all-start) | async-done | bytes 524320 | tf_op jit(solution)/shard_map/all_to_all | solution.py:33
  37.9 4.1 %all-to-all-start.2 = ((bf16[16,2,8192]{2,1,0:T(2,128)(2,1)}), bf16[16,2,8192]{2,1,0:T(2,128)(2,1)S(1)}, u32[]{:S(2)}, u32[]{:S(2)}) async-start(bf16[16,2,8192]{2,1,0:T(2,128)(2,1)} %reshape.74), calls=%async_computation.2 | async-start | bytes 1048576 | tf_op jit(solution)/shard_map/all_to_all | solution.py:54
  57.2 2.6 add_convert_fusion.3
  59.9 1.4 add_convert_fusion.2
  61.4 1.4 add_convert_fusion.1
  62.9 1.5 multiply_convert_fusion
  65.0 0.6 constant_dynamic-update-slice_fusion.14
  65.6 0.6 constant_dynamic-update-slice_fusion.13
  66.9 0.6 constant_dynamic-update-slice_fusion.11
  67.5 0.6 constant_dynamic-update-slice_fusion.10
  68.7 0.6 constant_dynamic-update-slice_fusion.8
  69.3 0.6 constant_dynamic-update-slice_fusion.7
  69.9 0.6 constant_dynamic-update-slice_fusion.6
  70.5 0.6 constant_dynamic-update-slice_fusion.5
  71.2 0.6 constant_dynamic-update-slice_fusion.4
  72.4 0.6 constant_dynamic-update-slice_fusion.2
  73.0 0.6 constant_dynamic-update-slice_fusion.1
  74.2 5.7 %all-to-all-start.1 = ((bf16[16,1,64,256]{3,2,1,0:T(8,128)(2,1)}), bf16[16,1,64,256]{3,2,1,0:T(8,128)(2,1)S(1)}, u32[]{:S(2)}, u32[]{:S(2)}) async-start(bf16[16,1,64,256]{3,2,1,0:T(8,128)(2,1)} %constant_dynamic-update-slice_fusion), calls=%async_computation.1 | async-start | bytes 1048576 | tf_op jit(solution)/shard_map/all_to_all | solution.py:44
  80.0 1.4 fusion.25
  81.8 0.9 copy-done.19
  83.1 0.6 fusion.28
  84.1 0.9 copy-done.23
  85.0 0.6 fusion.31
  86.1 0.9 copy-done.21
  87.0 0.6 fusion.34
  87.8 1.1 fusion.11
  89.0 1.5 convolution_bitcast_fusion.1
  90.5 3.9 %all-to-all-done.1 = bf16[16,1,64,256]{3,2,1,0:T(8,128)(2,1)S(1)} async-done(((bf16[16,1,64,256]{3,2,1,0:T(8,128)(2,1)}), bf16[16,1,64,256]{3,2,1,0:T(8,128)(2,1)S(1)}, u32[]{:S(2)}, u32[]{:S(2)}) %all-to-all-start.1) | async-done | bytes 524320 | tf_op jit(solution)/shard_map/all_to_all | solution.py:44
  94.4 4.1 %all-to-all-start.3 = ((bf16[16,64,256]{2,1,0:T(8,128)(2,1)}), bf16[16,64,256]{2,1,0:T(8,128)(2,1)S(1)}, u32[]{:S(2)}, u32[]{:S(2)}) async-start(bf16[16,64,256]{2,1,0:T(8,128)(2,1)} %fusion.11), calls=%async_computation.3 | async-start | bytes 1048576 | tf_op jit(solution)/shard_map/all_to_all | solution.py:74
  98.6 3.1 %convolution_bitcast_fusion.2 = f32[1,512,256]{2,1,0:T(8,128)} fusion(bf16[16,64,256]{2,1,0:T(8,128)(2,1)} %copy-done.7, bf16[16,64,256]{2,1,0:T(8,128)(2,1)} %copy-done.6, bf16[16,64,256]{2,1,0:T(8,128)(2,1)S(1)} %fusion.7, f32[16,64,256]{2,1,0:T(8,128)} %get-tuple-element.25), kind=kOutput, calls=%fused_computation.18 | convolution fusion | flops 273154048 | bytes 3145728 | tf_op jit(solution)/shard_map/tpk,tpd->kd/dot_general | solution.py:62
  101.8 1.5 convolution_bitcast_fusion.3
  103.3 1.0 fusion.22
  104.3 8.7 %all-to-all-done.3 = bf16[16,64,256]{2,1,0:T(8,128)(2,1)S(1)} async-done(((bf16[16,64,256]{2,1,0:T(8,128)(2,1)}), bf16[16,64,256]{2,1,0:T(8,128)(2,1)S(1)}, u32[]{:S(2)}, u32[]{:S(2)}) %all-to-all-start.3) | async-done | bytes 524320 | tf_op jit(solution)/shard_map/all_to_all | solution.py:74
  113.4 0.8 copy.19
  115.5 1.5 pad_maximum_fusion
  117.1 1.0 fusion.3
  118.1 42.8 %reduce-scatter.8.cloned.1.call-done = f32[16,128]{1,0:T(8,128)} async-done(((f32[256,128]{1,0:T(8,128)}), f32[16,128]{1,0:T(8,128)}) %reduce-scatter.8.cloned.1.call-update) | async-done | bytes 8208 | tf_op jit(solution)/shard_map/reduce_scatter | solution.py:80
  160.8 58.2 %reduce-scatter.10.cloned.1.call-done = f32[8,256]{1,0:T(8,128)} async-done(((f32[128,256]{1,0:T(8,128)}), f32[8,256]{1,0:T(8,128)}) %reduce-scatter.10.cloned.1.call-update) | async-done | bytes 8208
  219.0 64.9 %reduce-scatter.6.cloned.1.call-done = f32[4,32,256]{2,1,0:T(8,128)} async-done(((f32[4,512,256]{2,1,0:T(8,128)}), f32[4,32,256]{2,1,0:T(8,128)}) %reduce-scatter.6.cloned.1.call-update) | async-done | bytes 131088 | tf_op jit(solution)/shard_map/reduce_scatter | solution.py:73
  (79 shorter events, 9.8 us)
Async XLA Ops:
  7.2 16.3 %copy-start = (bf16[1,1024,128]{2,1,0:T(8,128)(2,1)S(1)}, bf16[1,1024,128]{2,1,0:T(8,128)(2,1)}, u32[]{:S(2)}) copy-start(bf16[1,1024,128]{2,1,0:T(8,128)(2,1)} %param.15) | copy-start | bytes 786436
  10.7 12.7 %copy-start.17 = (bf16[256,128]{1,0:T(8,128)(2,1)S(1)}, bf16[256,128]{1,0:T(8,128)(2,1)}, u32[]{:S(2)}) copy-start(bf16[256,128]{1,0:T(8,128)(2,1)} %param.14) | copy-start | bytes 196612
  16.0 21.9 %all-to-all-start = ((bf16[16,2,8192]{2,1,0:T(2,128)(2,1)}), bf16[16,2,8192]{2,1,0:T(2,128)(2,1)S(1)}, u32[]{:S(2)}, u32[]{:S(2)}) async-start(bf16[16,2,8192]{2,1,0:T(2,128)(2,1)} %reshape.76), calls=%async_computation | async-start | bytes 1048576 | tf_op jit(solution)/shard_map/all_to_all | solution.py:33
  24.6 17.4 %copy-start.20 = (s32[4]{0:T(128)S(1)}, s32[4]{0:T(128)}, u32[]{:S(2)}) copy-start(s32[4]{0:T(128)} %param.10) | copy-start | bytes 52
  37.9 18.6 %all-to-all-start.2 = ((bf16[16,2,8192]{2,1,0:T(2,128)(2,1)}), bf16[16,2,8192]{2,1,0:T(2,128)(2,1)S(1)}, u32[]{:S(2)}, u32[]{:S(2)}) async-start(bf16[16,2,8192]{2,1,0:T(2,128)(2,1)} %reshape.74), calls=%async_computation.2 | async-start | bytes 1048576 | tf_op jit(solution)/shard_map/all_to_all | solution.py:54
  57.2 2.6 copy-start.4
  57.2 2.7 copy-start.18
  59.8 3.0 %copy-start.6 = (bf16[16,64,256]{2,1,0:T(8,128)(2,1)}, bf16[16,64,256]{2,1,0:T(8,128)(2,1)S(1)}, u32[]{:S(2)}) copy-start(bf16[16,64,256]{2,1,0:T(8,128)(2,1)S(1)} %get-tuple-element.22) | copy-start | bytes 1572868
  59.9 3.0 %copy-start.7 = (bf16[16,64,256]{2,1,0:T(8,128)(2,1)}, bf16[16,64,256]{2,1,0:T(8,128)(2,1)S(1)}, u32[]{:S(2)}) copy-start(bf16[16,64,256]{2,1,0:T(8,128)(2,1)S(1)} %pad_dynamic-slice_fusion.6) | copy-start | bytes 1572868
  61.3 1.5 copy-start.8
  61.4 1.5 copy-start.10
  62.9 1.5 copy-start.2
  64.4 15.6 %copy-start.12 = (bf16[16,64,256]{2,1,0:T(8,128)(2,1)S(1)}, bf16[16,64,256]{2,1,0:T(8,128)(2,1)}, u32[]{:S(2)}) copy-start(bf16[16,64,256]{2,1,0:T(8,128)(2,1)} %get-tuple-element.16) | copy-start | bytes 1572868
  74.2 20.2 %all-to-all-start.1 = ((bf16[16,1,64,256]{3,2,1,0:T(8,128)(2,1)}), bf16[16,1,64,256]{3,2,1,0:T(8,128)(2,1)S(1)}, u32[]{:S(2)}, u32[]{:S(2)}) async-start(bf16[16,1,64,256]{3,2,1,0:T(8,128)(2,1)} %constant_dynamic-update-slice_fusion), calls=%async_computation.1 | async-start | bytes 1048576 | tf_op jit(solution)/shard_map/all_to_all | solution.py:44
  81.5 1.2 copy-start.19
  81.5 1.5 copy-start.24
  83.8 1.2 copy-start.23
  85.8 1.2 copy-start.21
  87.8 1.1 copy-start.9
  87.8 1.2 copy-start.11
  94.4 18.6 %all-to-all-start.3 = ((bf16[16,64,256]{2,1,0:T(8,128)(2,1)}), bf16[16,64,256]{2,1,0:T(8,128)(2,1)S(1)}, u32[]{:S(2)}, u32[]{:S(2)}) async-start(bf16[16,64,256]{2,1,0:T(8,128)(2,1)} %fusion.11), calls=%async_computation.3 | async-start | bytes 1048576 | tf_op jit(solution)/shard_map/all_to_all | solution.py:74
  98.5 62.3 %reduce-scatter.8.cloned.1.call-start = ((), (), s32[]{:S(2)}) async-start(), calls=%async_computation.8 | async-start | bytes 139264 | tf_op jit(solution)/shard_map/reduce_scatter | solution.py:80
  98.6 3.2 %copy-start.5 = (bf16[16,64,256]{2,1,0:T(8,128)(2,1)S(1)}, bf16[16,64,256]{2,1,0:T(8,128)(2,1)}, u32[]{:S(2)}) copy-start(bf16[16,64,256]{2,1,0:T(8,128)(2,1)} %copy-done.4) | copy-start | bytes 1572868
  98.6 3.2 %copy-start.22 = (f32[16,64,256]{2,1,0:T(8,128)S(1)}, f32[16,64,256]{2,1,0:T(8,128)}, u32[]{:S(2)}) copy-start(f32[16,64,256]{2,1,0:T(8,128)} %get-tuple-element.23) | copy-start | bytes 3145732
  101.8 11.2 %copy-start.1 = (bf16[1,1024,128]{2,1,0:T(8,128)(2,1)S(1)}, bf16[1,1024,128]{2,1,0:T(8,128)(2,1)}, u32[]{:S(2)}) copy-start(bf16[1,1024,128]{2,1,0:T(8,128)(2,1)} %param.8) | copy-start | bytes 786436
  103.3 10.9 %copy-start.3 = (bf16[16,64,256]{2,1,0:T(8,128)(2,1)S(1)}, bf16[16,64,256]{2,1,0:T(8,128)(2,1)}, u32[]{:S(2)}) copy-start(bf16[16,64,256]{2,1,0:T(8,128)(2,1)} %copy-done.2) | copy-start | bytes 1572868
  103.3 10.9 %copy-start.13 = (bf16[16,64,256]{2,1,0:T(8,128)(2,1)S(1)}, bf16[16,64,256]{2,1,0:T(8,128)(2,1)}, u32[]{:S(2)}) copy-start(bf16[16,64,256]{2,1,0:T(8,128)(2,1)} %get-tuple-element.16) | copy-start | bytes 1572868
  104.3 114.8 %reduce-scatter.10.cloned.1.call-start = ((), (), s32[]{:S(2)}) async-start(), calls=%async_computation.9 | async-start | bytes 139264
  114.1 1.0 copy-start.14
  114.1 169.8 %reduce-scatter.6.cloned.1.call-start = ((), (), s32[]{:S(2)}) async-start(), calls=%async_computation.7 | async-start | bytes 2228224 | tf_op jit(solution)/shard_map/reduce_scatter | solution.py:73
  114.2 1.1 copy-start.15
  114.2 1.3 copy-start.16
Sparse Core Ops, SparseCore 0:
  104.4 56.3 reduce-scatter.7
  164.9 54.1 reduce-scatter.9
  223.4 60.5 reduce-scatter.5
